TPU v7x, 32 devices: a whole 2x2x4 slice. The times are simulated.
32 devices in a mesh: wide: 8 (over z, x), narrow: 4 (over y, core).
Axes of the slice: x: 2, y: 2, z: 4, core: 2. Of those that a mesh axis runs over, the one named last changes fastest.
Arguments:
- a_blocks: bfloat16 [32, 8, 2, 128, 128], P('wide', 'narrow'), may hold values from -0.125 to 0.125
- a_cols: int32 [32, 8, 2], P('wide'), may hold values from 0 to 1
- a_scales: float32 [32, 8, 2], P('wide'), may hold values from 0.3 to 3
- a_counts: int32 [32, 8], P('wide'), may hold values from 0 to 2
- b_panel: bfloat16 [2048, 1024], P('wide', 'narrow'), may hold values from -6 to 6
- b_scales: float32 [16], replicated, may hold values from 0.3 to 3
- keep_mask: int32 [32, 8], P('wide', 'narrow'), may hold values 0 or 1
- row_perm: int32 [8, 4], P('wide'), may hold values from 0 to 3, each once within a row
Outputs:
- relaid: bfloat16 [4096, 1024], P(('wide', 'narrow'))
Inputs may be any that keep to these rules, and one draw needn't show every extreme that they name: `a_counts`: slots at or beyond the count hold no block of the operand. `row_perm`: each row holds every number from 0 to 3 once.
All inputs are finite; a program needn't handle non-finite values. No bound on the sum of `keep_mask` on one device may be relied on, other than what follows from the above.
Results may differ from a plain program's by a relative error of at most 0.0049.
Values may be sent and summed in bfloat16 or wider, within the bound.
A program may use at most 64 MiB of HBM per device.

v0:
```python
import functools

import jax
import jax.numpy as jnp
from jax import lax
from jax.experimental import pallas as pl
from jax.experimental.pallas import tpu as pltpu
from jax.sharding import PartitionSpec as P

MESH = pl.DeviceIdType.MESH
HALVES = 2


def kernel(
    wide_count,
    a_hbm,
    cols_hbm,
    scales_hbm,
    counts_hbm,
    b_hbm,
    b_scales_hbm,
    keep_hbm,
    perm_hbm,
    out,
    cols,
    scales,
    counts,
    b_scales,
    keep,
    perm,
    table_sem,
    a_own,
    left,
    right,
    result,
    partial,
    load_sem,
    b_recv,
    b_up,
    b_down,
    b_cross,
    a_recv,
    a_mate,
    a_far,
    r_send,
    r_recv,
):
    w = lax.axis_index("wide")
    n = lax.axis_index("narrow")
    x = w % 2
    z = w // 2
    depth = wide_count // 2
    rows, share, slots, side = a_own.shape[:4]
    kb = b_hbm.shape[0] // side
    width = b_hbm.shape[1]
    part = b_hbm.shape[0] // HALVES
    across = w + 1 - 2 * x
    mate = n + 1 - 2 * (n % 2)
    far = (n + 2) % 4
    diagonal = 3 - n

    tables = [
        pltpu.make_async_copy(source, kept, table_sem.at[i])
        for i, (source, kept) in enumerate(
            (
                (perm_hbm, perm),
                (cols_hbm, cols),
                (scales_hbm, scales),
                (counts_hbm, counts),
                (b_scales_hbm, b_scales),
                (keep_hbm, keep),
            )
        )
    ]
    for copy in tables:
        copy.start()
    load_a = pltpu.make_async_copy(a_hbm, a_own, load_sem.at[0])
    load_a.start()
    load_b = [
        pltpu.make_async_copy(
            b_hbm.at[pl.ds(h * part, part)], right.at[w * HALVES + h], load_sem.at[1 + h]
        )
        for h in range(HALVES)
    ]
    for copy in load_b:
        copy.start()

    barrier = pltpu.get_barrier_semaphore()
    for peer in ((w, mate), (w, far), (w, diagonal), (across, n)):
        pl.semaphore_signal(barrier, inc=1, device_id=peer, device_id_type=MESH)

    @pl.when(z > 0)
    def _():
        pl.semaphore_signal(barrier, inc=1, device_id=(w - 2, n), device_id_type=MESH)

    @pl.when(z < depth - 1)
    def _():
        pl.semaphore_signal(barrier, inc=1, device_id=(w + 2, n), device_id_type=MESH)

    neighbours = jnp.where(z > 0, 1, 0) + jnp.where(z < depth - 1, 1, 0)
    pl.semaphore_wait(barrier, 4 + neighbours)

    def piece(source, slot, sent, target):
        return pltpu.make_async_remote_copy(
            src_ref=source,
            dst_ref=right.at[slot],
            send_sem=sent.at[slot],
            recv_sem=b_recv.at[slot],
            device_id=(target, n),
            device_id_type=MESH,
        )

    def upward(slot, source=None):
        return piece(right.at[slot] if source is None else source, slot, b_up, w + 2)

    def downward(slot, source=None):
        return piece(right.at[slot] if source is None else source, slot, b_down, w - 2)

    def crossing(slot, source=None):
        return piece(right.at[slot] if source is None else source, slot, b_cross, across)

    for h in range(HALVES):
        own = w * HALVES + h
        source = b_hbm.at[pl.ds(h * part, part)]

        @pl.when(z < depth - 1)
        def _():
            upward(own, source).start()

        @pl.when(z > 0)
        def _():
            downward(own, source).start()

        crossing(own, source).start()

    def block(origin, q, sent, target):
        return pltpu.make_async_remote_copy(
            src_ref=left.at[origin, q],
            dst_ref=left.at[origin, q],
            send_sem=sent,
            recv_sem=a_recv.at[origin, q],
            device_id=(w, target),
            device_id_type=MESH,
        )

    def home(q):
        total = jnp.int32(0)
        for r in range(rows):
            total = jnp.where(perm[0, r] == q, r, total)
        return total

    for copy in tables:
        copy.wait()
    load_a.wait()
    sent_order = (n, mate, diagonal, far)
    for q in sent_order:
        r = home(q)
        for j in range(share):
            s = n * share + j
            panel = (w - s + wide_count) % wide_count
            weights, places = [], []
            for m in range(slots):
                place = cols[r, m, s]
                live = jnp.where(m < counts[r, s], 1.0, 0.0)
                weights.append(scales[r, m, s] * b_scales[panel * kb + place] * live)
                places.append(place)
            for k in range(kb):
                total = None
                for m in range(slots):
                    weight = jnp.where(places[m] == k, weights[m], 0.0)
                    term = a_own[r, j, m].astype(jnp.float32) * weight
                    total = term if total is None else total + term
                left[n, q, j, :, k * side : (k + 1) * side] = total.astype(jnp.bfloat16)
        block(n, q, a_far.at[q], far).start()
        block(n, q, a_mate.at[0, q], mate).start()

    for step in range(1, max(depth, rows + 1)):
        if step < depth:
            for h in range(HALVES):
                from_below = (w - 2 * step) * HALVES + h
                from_above = (w + 2 * step) * HALVES + h

                @pl.when(z - step >= 0)
                def _():
                    upward(from_below).wait_recv()

                    @pl.when(z < depth - 1)
                    def _():
                        upward(from_below).start()

                    crossing(from_below).start()

                @pl.when(z + step < depth)
                def _():
                    downward(from_above).wait_recv()

                    @pl.when(z > 0)
                    def _():
                        downward(from_above).start()

                    crossing(from_above).start()

        if step <= rows:
            q = (far, diagonal, mate, n)[step - 1]
            block(far, q, a_far.at[q], far).wait_recv()
            block(far, q, a_mate.at[1, q], mate).start()

    for copy in load_b:
        copy.wait()
    for q in (far, diagonal, mate, n):
        block(mate, q, a_mate.at[0, q], mate).wait_recv()
    for q in (far, diagonal, mate, n):
        block(diagonal, q, a_mate.at[1, q], mate).wait_recv()

    def panel_product(panel, rows_left):
        s = (w - panel + wide_count) % wide_count
        tile = right[pl.ds(panel * HALVES, HALVES)].reshape(kb * side, width)
        return jnp.dot(rows_left(s // share, s % share), tile, preferred_element_type=jnp.float32)

    for level in range(depth):
        product = panel_product(
            2 * level + x, lambda o, j: left[o, :, j].reshape(rows * side, kb * side)
        ).reshape(rows, side, width)
        partial[...] = product if level == 0 else partial[...] + product
    lower = z < depth // 2
    levels = []
    for turn in range(depth):
        levels.append(jnp.where(lower, turn, depth - 1 - turn))
    near = jnp.where((z == 0) | (z == depth - 1), 0, 1)
    levels[0], levels[1] = (
        jnp.where(near == 0, levels[0], levels[1]),
        jnp.where(near == 0, levels[1], levels[0]),
    )

    def peer_arrived(level):
        for h in range(HALVES):
            crossing((2 * level + 1 - x) * HALVES + h).wait_recv()

    for level in levels[:-1]:
        peer_arrived(level)
        partial[...] = partial[...] + panel_product(
            2 * level + 1 - x, lambda o, j: left[o, :, j].reshape(rows * side, kb * side)
        ).reshape(rows, side, width)
    peer_arrived(levels[-1])

    columns = pl.ds(pl.multiple_of(n * width, width), width)

    def deliver(q):
        return pltpu.make_async_remote_copy(
            src_ref=result.at[q],
            dst_ref=out.at[:, columns],
            send_sem=r_send.at[q],
            recv_sem=r_recv.at[n],
            device_id=(w, q),
            device_id_type=MESH,
        )

    for q in (far, diagonal, mate, n):
        total = partial[q] + panel_product(
            2 * levels[-1] + 1 - x, lambda o, j: left[o, q, j]
        )
        r = home(q)
        kept = []
        for c in range(width // side):
            kept.append(
                total[:, c * side : (c + 1) * side] * keep[c, r].astype(jnp.float32)
            )
        filtered = jnp.concatenate(kept, axis=1).astype(jnp.bfloat16)
        if q is n:
            out[:, columns] = filtered
        else:
            result[q] = filtered
            deliver(q).start()

    for q in (far, diagonal, mate):
        deliver(q).wait_send()
    for q in sent_order:
        block(n, q, a_far.at[q], far).wait_send()
        block(n, q, a_mate.at[0, q], mate).wait_send()
        block(far, q, a_mate.at[1, q], mate).wait_send()
    for h in range(HALVES):
        for step in range(depth):
            from_below = (w - 2 * step) * HALVES + h
            from_above = (w + 2 * step) * HALVES + h

            @pl.when(z - step >= 0)
            def _():
                @pl.when(z < depth - 1)
                def _():
                    upward(from_below).wait_send()

                crossing(from_below).wait_send()

            @pl.when((z + step < depth) & (z > 0))
            def _():
                downward(from_above).wait_send()

            if step > 0:

                @pl.when(z + step < depth)
                def _():
                    crossing(from_above).wait_send()

    for origin in (mate, far, diagonal):
        source_columns = pl.ds(pl.multiple_of(origin * width, width), width)
        pltpu.make_async_remote_copy(
            src_ref=result.at[origin],
            dst_ref=out.at[:, source_columns],
            send_sem=r_send.at[origin],
            recv_sem=r_recv.at[origin],
            device_id=(w, origin),
            device_id_type=MESH,
        ).wait_recv()


def fused(wide_count, a_blocks, a_cols, a_scales, a_counts, b_panel, b_scales, keep_mask, row_perm):
    rows, share, slots, side = a_blocks.shape[:4]
    depth, width = b_panel.shape
    narrow_count = 4
    pieces = wide_count * HALVES
    in_place = pl.BlockSpec(memory_space=pltpu.HBM)
    dma = pltpu.SemaphoreType.DMA
    return pl.pallas_call(
        functools.partial(kernel, wide_count),
        out_shape=jax.ShapeDtypeStruct((side, width * narrow_count), jnp.bfloat16),
        in_specs=[in_place] * 8,
        out_specs=pl.BlockSpec(memory_space=pltpu.VMEM),
        scratch_shapes=[
            pltpu.SMEM((rows, slots, a_cols.shape[1]), jnp.int32),
            pltpu.SMEM((rows, slots, a_cols.shape[1]), jnp.float32),
            pltpu.SMEM(a_counts.shape, jnp.int32),
            pltpu.SMEM(b_scales.shape, jnp.float32),
            pltpu.SMEM((keep_mask.shape[1], rows), jnp.int32),
            pltpu.SMEM(row_perm.shape, jnp.int32),
            dma((6,)),
            pltpu.VMEM(a_blocks.shape, jnp.bfloat16),
            pltpu.VMEM((narrow_count, rows, share, side, depth), jnp.bfloat16),
            pltpu.VMEM((pieces, depth // HALVES, width), jnp.bfloat16),
            pltpu.VMEM((narrow_count, side, width), jnp.bfloat16),
            pltpu.VMEM((rows, side, width), jnp.float32),
            dma((1 + HALVES,)),
            dma((pieces,)),
            dma((pieces,)),
            dma((pieces,)),
            dma((pieces,)),
            dma((narrow_count, rows)),
            dma((2, rows)),
            dma((rows,)),
            dma((narrow_count,)),
            dma((narrow_count,)),
        ],
        compiler_params=pltpu.CompilerParams(
            collective_id=0, has_side_effects=True, vmem_limit_bytes=60 * 2**20
        ),
    )(
        a_blocks,
        jnp.transpose(a_cols, (0, 2, 1)),
        jnp.transpose(a_scales, (0, 2, 1)),
        a_counts,
        b_panel,
        b_scales,
        jnp.transpose(keep_mask),
        row_perm,
    )


def shifted(block, axis, distance):
    devices = range(lax.axis_size(axis))
    route = [((i - distance) % len(devices), i) for i in devices]
    return lax.ppermute(block, axis, route)


def chosen(table, index):
    tail = (1,) * (table.ndim - 1)
    index = index.reshape(index.shape + tail)
    found = jnp.broadcast_to(table[0], index.shape[: index.ndim - len(tail)] + table.shape[1:])
    for k in range(1, table.shape[0]):
        found = jnp.where(index == k, table[k], found)
    return found


def section_term(row_blocks, slot_cols, weights, b_tiles):
    row_count = row_blocks.shape[0]
    slot_count = row_blocks.shape[1]
    block_side = row_blocks.shape[2]
    scaled = (row_blocks.astype(jnp.float32) * weights[:, :, None, None]).astype(jnp.bfloat16)
    left = jnp.transpose(scaled, (0, 2, 1, 3)).reshape(
        row_count, block_side, slot_count * block_side
    )
    right = chosen(b_tiles, slot_cols.reshape(-1)).reshape(
        row_count, slot_count * block_side, b_tiles.shape[2]
    )
    return jnp.einsum("rik,rkj->rij", left, right, preferred_element_type=jnp.float32)


def by_rings(a_blocks, a_cols, a_scales, a_counts, b_panel, b_scales, keep_mask, row_perm):
    wide_count = lax.axis_size("wide")
    narrow_count = lax.axis_size("narrow")
    device_row = lax.axis_index("wide")
    device_column = lax.axis_index("narrow")
    row_count, section_share, slot_count, block_side = a_blocks.shape[:4]
    section_total = section_share * narrow_count
    k_rows = b_panel.shape[0] // block_side
    out_width = b_panel.shape[1]
    col_blocks = out_width // block_side
    held = [a_blocks]
    for _ in range(narrow_count - 1):
        held.append(shifted(held[-1], "narrow", 1))
    held = jnp.stack(held)
    slot_ids = jnp.arange(slot_count, dtype=jnp.int32)
    accumulated = jnp.zeros((row_count, block_side, out_width), jnp.float32)
    current = b_panel.reshape(k_rows, block_side, out_width)
    for step_number in range(section_total):
        if step_number > 0:
            current = shifted(current, "wide", 1)
        back = (device_column - step_number // section_share) % narrow_count
        row_blocks = lax.dynamic_index_in_dim(held, back, keepdims=False)
        row_blocks = row_blocks[:, step_number % section_share]
        panel_number = (device_row - step_number) % wide_count
        slot_cols = a_cols[:, step_number]
        live_slots = (slot_ids[None, :] < a_counts[:, step_number][:, None]).astype(jnp.float32)
        weights = (
            a_scales[:, step_number]
            * chosen(lax.dynamic_slice(b_scales, (panel_number * k_rows,), (k_rows,)), slot_cols)
            * live_slots
        )
        accumulated = accumulated + section_term(row_blocks, slot_cols, weights, current)
    masked = (
        accumulated.reshape(row_count, block_side, col_blocks, block_side)
        * keep_mask.astype(jnp.float32)[:, None, :, None]
    )
    filtered = masked.astype(jnp.bfloat16).reshape(row_count, block_side, out_width)
    new_order = row_perm[0]
    positions = jnp.arange(row_count, dtype=jnp.int32)
    matches = (new_order[None, :] == positions[:, None]).astype(jnp.int32)
    inverse = jnp.sum(positions[None, :] * matches, axis=1)
    reordered = chosen(filtered, inverse).reshape(row_count * block_side, out_width)
    return lax.all_to_all(reordered, "narrow", split_axis=0, concat_axis=1, tiled=True)


def per_device(*operands):
    wide_count = lax.axis_size("wide")
    narrow_count = lax.axis_size("narrow")
    rows, share = operands[0].shape[:2]
    if narrow_count == 4 and rows == 4 and wide_count == share * narrow_count == 8:
        return fused(wide_count, *operands)
    return by_rings(*operands)


def solution(mesh):
    in_specs = (
        P("wide", "narrow", None, None, None),
        P("wide", None, None),
        P("wide", None, None),
        P("wide", None),
        P("wide", "narrow"),
        P(),
        P("wide", "narrow"),
        P("wide", None),
    )
    out_specs = P(("wide", "narrow"), None)
    return jax.shard_map(
        per_device, mesh=mesh, in_specs=in_specs, out_specs=out_specs, check_vma=False
    )
```

profile of v0, /device:TPU:0, one launch (start us, length us, event | category | flops | bytes accessed | tf_op | source)
XLA Modules:
  0.0 26.5 jit_solution(94528815972979820)
XLA Ops:
  0.0 24.8 %shard_map.82 = bf16[128,1024]{1,0:T(8,128)(2,1)} custom-call(bf16[4,2,2,128,128]{4,3,2,1,0:T(8,128)(2,1)} %a_hbm.1, s32[4,2,8]{2,1,0:T(2,128)} %bitcast.3, f32[4,2,8]{2,1,0:T(2,128)} %bitcast.4, s32[4,8]{1,0:T(4,128)} %counts_hbm.1, bf16[256,256]{1,0:T(8,128)(2,1)} %b_hbm.1, f32[16]{0:T(128)} %b_scales_hbm.1, s32[2,4]{1,0:T(2,128)} %bitcast.5, s32[1,4]{1,0:T(1,128)} %perm_hbm.1), custom_call_target="tpu_custom_call" | custom-call | tf_op jit(solution)/shard_map/pallas_call | solution.py:323
  24.8 1.7 %copy.10 = bf16[128,1024]{1,0:T(8,128)(2,1)} copy(bf16[128,1024]{1,0:T(8,128)(2,1)} %shard_map.82) | data formatting | bytes 524288
where the time goes:
time: 26.7 us; the launch traced here: 26.5 us
  Pallas kernels  24.8 us (93%)
  local copies, waits for them, and re-layouts  1.67 us (6%)
    pallas_call x1, Pallas kernels, fused(): pl.pallas_call(functools.partial(kernel, wide_count), out_shape=jax.Shape...  24.8 us
    unnamed x1, local copies, waits for them, and re-layouts  1.67 us

commit v1 on v0

--- a/solution.py
+++ b/solution.py
@@ -322,7 +322,7 @@
     dma = pltpu.SemaphoreType.DMA
     return pl.pallas_call(
         functools.partial(kernel, wide_count),
-        out_shape=jax.ShapeDtypeStruct((side, width * narrow_count), jnp.bfloat16),
+        out_shape=pltpu.VMEM((side, width * narrow_count), jnp.bfloat16),
         in_specs=[in_place] * 8,
         out_specs=pl.BlockSpec(memory_space=pltpu.VMEM),
         scratch_shapes=[

time: 26.7 us -> 25.1 us (0.940)
  local copies, waits for them, and re-layouts: 1.67 us -> 0.71 us
  Pallas kernels: 24.8 us -> 24.1 us
    unnamed x1, local copies, waits for them, and re-layouts: 1.67 us -> 0.71 us
    pallas_call x1, Pallas kernels: 24.8 us -> 24.1 us  [fused(): pl.pallas_call(functools.partial(kernel, wide_count), out_shape=pltpu.VME...]
where the time goes in v1:
time: 25.1 us; the launch traced here: 24.9 us
  Pallas kernels  24.1 us (96%)
  local copies, waits for them, and re-layouts  0.71 us (3%)
    pallas_call x1, Pallas kernels, fused(): pl.pallas_call(functools.partial(kernel, wide_count), out_shape=pltpu.VME...  24.1 us
    unnamed x1, local copies, waits for them, and re-layouts  0.71 us

profile of v1, /device:TPU:0, one launch (start us, length us, event | category | flops | bytes accessed | tf_op | source)
XLA Modules:
  0.0 24.9 jit_solution(4960812059864986465)
XLA Ops:
  0.0 24.1 %shard_map.82 = bf16[128,1024]{1,0:T(8,128)(2,1)S(1)} custom-call(bf16[4,2,2,128,128]{4,3,2,1,0:T(8,128)(2,1)} %a_hbm.1, s32[4,2,8]{2,1,0:T(2,128)} %bitcast.3, f32[4,2,8]{2,1,0:T(2,128)} %bitcast.4, s32[4,8]{1,0:T(4,128)} %counts_hbm.1, bf16[256,256]{1,0:T(8,128)(2,1)} %b_hbm.1, f32[16]{0:T(128)} %b_scales_hbm.1, s32[2,4]{1,0:T(2,128)} %bitcast.5, ...), custom_call_target="tpu_custom_call" | custom-call | tf_op jit(solution)/shard_map/pallas_call | solution.py:323
  24.1 0.7 %copy.10 = bf16[128,1024]{1,0:T(8,128)(2,1)} copy(bf16[128,1024]{1,0:T(8,128)(2,1)S(1)} %shard_map.82) | data formatting | bytes 524288

commit v2 on v1

v2 whole, which is shorter than its diff:
```python
import functools

import jax
import jax.numpy as jnp
from jax import lax
from jax.experimental import pallas as pl
from jax.experimental.pallas import tpu as pltpu
from jax.sharding import PartitionSpec as P

MESH = pl.DeviceIdType.MESH
HALVES = 2
PARTS = 4
WIDE = 8
DEPTH = 4
NARROW = 4
EARLY = 1


def kernel(
    a_hbm,
    cols_hbm,
    scales_hbm,
    counts_hbm,
    b_hbm,
    b_scales_hbm,
    keep_hbm,
    perm_hbm,
    out,
    cols,
    scales,
    counts,
    b_scales,
    keep,
    perm,
    table_sem,
    a_own,
    left,
    right,
    result,
    total,
    load_sem,
    b_recv,
    b_up,
    b_down,
    b_cross,
    a_recv,
    a_mate,
    a_far,
    r_send,
    r_recv,
):
    w = lax.axis_index("wide")
    n = lax.axis_index("narrow")
    x = w % 2
    z = w // 2
    y = n // 2
    core = n % 2
    rows, share, slots, side = a_own.shape[:4]
    kb = b_hbm.shape[0] // side
    width = b_hbm.shape[1]
    across = w + 1 - 2 * x
    mate = n + 1 - 2 * core
    far = (n + 2) % 4
    diagonal = 3 - n

    barrier = pltpu.get_barrier_semaphore()
    for peer in ((w, mate), (w, far), (w, diagonal), (across, n)):
        pl.semaphore_signal(barrier, inc=1, device_id=peer, device_id_type=MESH)

    @pl.when(z > 0)
    def _():
        pl.semaphore_signal(barrier, inc=1, device_id=(w - 2, n), device_id_type=MESH)

    @pl.when(z < DEPTH - 1)
    def _():
        pl.semaphore_signal(barrier, inc=1, device_id=(w + 2, n), device_id_type=MESH)

    tables = [
        pltpu.make_async_copy(source, kept, table_sem.at[i])
        for i, (source, kept) in enumerate(
            (
                (perm_hbm, perm),
                (cols_hbm, cols),
                (scales_hbm, scales),
                (counts_hbm, counts),
                (b_scales_hbm, b_scales),
                (keep_hbm, keep),
            )
        )
    ]
    for copy in tables:
        copy.start()
    load_a = pltpu.make_async_copy(a_hbm, a_own, load_sem.at[0])
    load_a.start()
    load_b = [
        pltpu.make_async_copy(
            b_hbm.at[t % kb * side : (t % kb + 1) * side, t // kb * side : (t // kb + 1) * side],
            right.at[w * PARTS + t],
            load_sem.at[1 + t],
        )
        for t in range(PARTS)
    ]
    for copy in load_b:
        copy.start()

    def piece(slot, sent, target):
        return pltpu.make_async_remote_copy(
            src_ref=right.at[slot],
            dst_ref=right.at[slot],
            send_sem=sent.at[slot],
            recv_sem=b_recv.at[slot],
            device_id=(target, n),
            device_id_type=MESH,
        )

    def upward(slot):
        return piece(slot, b_up, w + 2)

    def downward(slot):
        return piece(slot, b_down, w - 2)

    def crossing(slot):
        return piece(slot, b_cross, across)

    def block(origin, pair, j, sent, target):
        return pltpu.make_async_remote_copy(
            src_ref=left.at[origin, pair, j],
            dst_ref=left.at[origin, pair, j],
            send_sem=sent,
            recv_sem=a_recv.at[origin, pair, j],
            device_id=(w, target),
            device_id_type=MESH,
        )

    def to_far(pair, j):
        return block(n, pair, j, a_far.at[pair, j], far)

    def to_mate(pair, j):
        return block(n, pair, j, a_mate.at[0, pair, j], mate)

    def from_far(pair, j):
        return block(far, pair, j, a_far.at[pair, j], far)

    def pass_on(pair, j):
        return block(far, pair, j, a_mate.at[1, pair, j], mate)

    def home(q):
        found = jnp.int32(0)
        for r in range(rows):
            found = jnp.where(perm[0, r] == q, r, found)
        return found

    def scale(pair, j):
        s = n * share + j
        panel = (w - s + WIDE) % WIDE
        for c in range(2):
            r = home(2 * pair + c)
            weights, places = [], []
            for m in range(slots):
                place = cols[r, m, s]
                live = jnp.where(m < counts[r, s], 1.0, 0.0)
                weights.append(scales[r, m, s] * b_scales[panel * kb + place] * live)
                places.append(place)
            for k in range(kb):
                value = None
                for m in range(slots):
                    weight = jnp.where(places[m] == k, weights[m], 0.0)
                    term = a_own[r, j, m].astype(jnp.float32) * weight
                    value = term if value is None else value + term
                left[n, pair, j, c * side : (c + 1) * side, k * side : (k + 1) * side] = (
                    value.astype(jnp.bfloat16)
                )

    pairs = (y, 1 - y)
    units = [(pair, j) for pair in pairs for j in range(share)]
    for copy in tables:
        copy.wait()
    load_a.wait()
    for unit in units[:EARLY]:
        scale(*unit)
    for copy in load_b:
        copy.wait()

    neighbours = jnp.where(z > 0, 1, 0) + jnp.where(z < DEPTH - 1, 1, 0)
    pl.semaphore_wait(barrier, 4 + neighbours)

    for unit in units[:EARLY]:
        to_far(*unit).start()
    for t in range(PARTS):
        own = w * PARTS + t
        crossing(own).start()

        @pl.when(z < DEPTH - 1)
        def _():
            upward(own).start()

        @pl.when(z > 0)
        def _():
            downward(own).start()

    for unit in units[:EARLY]:
        to_mate(*unit).start()
    for unit in units[EARLY:]:
        scale(*unit)
        to_far(*unit).start()
        to_mate(*unit).start()

    def relay(step, t):
        from_below = (w - 2 * step) * PARTS + t
        from_above = (w + 2 * step) * PARTS + t

        @pl.when(z - step >= 0)
        def _():
            upward(from_below).wait_recv()

            @pl.when(z < DEPTH - 1)
            def _():
                upward(from_below).start()

            crossing(from_below).start()

        @pl.when(z + step < DEPTH)
        def _():
            downward(from_above).wait_recv()

            @pl.when(z > 0)
            def _():
                downward(from_above).start()

            crossing(from_above).start()

    def hand_over(pair, j):
        from_far(pair, j).wait_recv()
        pass_on(pair, j).start()

    def mate_arrived(pair, j):
        block(mate, pair, j, a_mate.at[0, pair, j], mate).wait_recv()

    def diagonal_arrived(pair, j):
        block(diagonal, pair, j, a_mate.at[1, pair, j], mate).wait_recv()

    near = (
        z,
        jnp.where(z == 0, 1, z - 1),
        jnp.where(z == 0, 2, jnp.where(z == 3, 1, z + 1)),
        jnp.where(z < 2, 3, 0),
    )

    def peer_arrived(level, h):
        for t in range(h * kb, h * kb + kb):
            crossing((2 * level + 1 - x) * PARTS + t).wait_recv()

    def half(panel, h):
        return right[pl.ds(panel * PARTS + h * kb, kb)].reshape(kb * side, side)

    def term(pair, j, level, h):
        panel = 2 * level + (x if j == 0 else 1 - x)
        origin = ((w - panel + WIDE) % WIDE) // share
        if h is None:
            tile = jnp.concatenate([half(panel, i) for i in range(HALVES)], axis=1)
        else:
            tile = half(panel, h)
        return jnp.dot(left[origin, pair, j], tile, preferred_element_type=jnp.float32)

    def add(slot, pair, terms, first=False):
        value = None
        for j, level in terms:
            product = term(pair, j, near[level], None)
            value = product if value is None else value + product
        total[slot] = value if first else total[slot] + value

    give, hold = 1 - y, y

    def deliver(c, h, source, target):
        start = pl.multiple_of(n * width + h * side, side)
        return pltpu.make_async_remote_copy(
            src_ref=result.at[source, c, h],
            dst_ref=out.at[:, pl.ds(start, side)],
            send_sem=r_send.at[source, c, h],
            recv_sem=r_recv.at[n, h],
            device_id=(w, target),
            device_id_type=MESH,
        )

    for t in range(PARTS):
        relay(1, t)
    hand_over(give, 0)
    relay(2, 0)
    relay(2, 1)
    hand_over(give, 1)
    relay(2, 2)
    relay(2, 3)
    mate_arrived(give, 0)
    mate_arrived(give, 1)
    diagonal_arrived(give, 0)
    add(0, give, [(0, 0), (0, 1), (0, 2)], first=True)
    relay(3, 0)
    relay(3, 1)
    diagonal_arrived(give, 1)
    for level in range(2):
        for h in range(HALVES):
            peer_arrived(near[level], h)
    add(0, give, [(1, 0), (1, 1)])
    hand_over(hold, 0)
    relay(3, 2)
    relay(3, 3)
    add(0, give, [(0, 3)])
    for h in range(HALVES):
        peer_arrived(near[2], h)
    add(0, give, [(1, 2)])
    mate_arrived(hold, 0)
    mate_arrived(hold, 1)
    diagonal_arrived(hold, 0)
    add(1, hold, [(0, 0), (0, 1), (0, 2), (0, 3)], first=True)
    for h in range(HALVES):
        peer_arrived(near[3], h)
        value = total[0, :, h * side : (h + 1) * side] + term(give, 1, near[3], h)
        for c in range(2):
            q = 2 * give + c
            kept = value[c * side : (c + 1) * side] * keep[h, home(q)].astype(jnp.float32)
            result[0, c, h] = kept.astype(jnp.bfloat16)
            deliver(c, h, 0, q).start()
    hand_over(hold, 1)
    diagonal_arrived(hold, 1)
    add(1, hold, [(1, 0), (1, 1), (1, 2), (1, 3)])
    for h in range(HALVES):
        c = 1 - core
        kept = total[1, pl.ds(pl.multiple_of(c * side, side), side), h * side : (h + 1) * side]
        result[1, 0, h] = (kept * keep[h, home(mate)].astype(jnp.float32)).astype(jnp.bfloat16)
        deliver(0, h, 1, mate).start()
    for h in range(HALVES):
        kept = total[1, pl.ds(pl.multiple_of(core * side, side), side), h * side : (h + 1) * side]
        start = pl.multiple_of(n * width + h * side, side)
        out[:, pl.ds(start, side)] = (kept * keep[h, home(n)].astype(jnp.float32)).astype(
            jnp.bfloat16
        )

    for unit in units:
        to_far(*unit).wait_send()
        to_mate(*unit).wait_send()
        pass_on(*unit).wait_send()
    for t in range(PARTS):
        for step in range(DEPTH):
            from_below = (w - 2 * step) * PARTS + t
            from_above = (w + 2 * step) * PARTS + t

            @pl.when(z - step >= 0)
            def _():
                @pl.when(z < DEPTH - 1)
                def _():
                    upward(from_below).wait_send()

                crossing(from_below).wait_send()

            @pl.when((z + step < DEPTH) & (z > 0))
            def _():
                downward(from_above).wait_send()

            if step > 0:

                @pl.when(z + step < DEPTH)
                def _():
                    crossing(from_above).wait_send()

    for h in range(HALVES):
        for c in range(2):
            deliver(c, h, 0, 2 * give + c).wait_send()
        deliver(0, h, 1, mate).wait_send()
    for origin in (mate, far, diagonal):
        for h in range(HALVES):
            start = pl.multiple_of(origin * width + h * side, side)
            pltpu.make_async_remote_copy(
                src_ref=result.at[0, 0, h],
                dst_ref=out.at[:, pl.ds(start, side)],
                send_sem=r_send.at[0, 0, h],
                recv_sem=r_recv.at[origin, h],
                device_id=(w, origin),
                device_id_type=MESH,
            ).wait_recv()


def fused(a_blocks, a_cols, a_scales, a_counts, b_panel, b_scales, keep_mask, row_perm):
    rows, share, slots, side = a_blocks.shape[:4]
    depth, width = b_panel.shape
    pieces = WIDE * PARTS
    in_place = pl.BlockSpec(memory_space=pltpu.HBM)
    dma = pltpu.SemaphoreType.DMA
    return pl.pallas_call(
        kernel,
        out_shape=pltpu.VMEM((side, width * NARROW), jnp.bfloat16),
        in_specs=[in_place] * 8,
        out_specs=pl.BlockSpec(memory_space=pltpu.VMEM),
        scratch_shapes=[
            pltpu.SMEM((rows, slots, a_cols.shape[1]), jnp.int32),
            pltpu.SMEM((rows, slots, a_cols.shape[1]), jnp.float32),
            pltpu.SMEM(a_counts.shape, jnp.int32),
            pltpu.SMEM(b_scales.shape, jnp.float32),
            pltpu.SMEM((keep_mask.shape[1], rows), jnp.int32),
            pltpu.SMEM(row_perm.shape, jnp.int32),
            dma((6,)),
            pltpu.VMEM(a_blocks.shape, jnp.bfloat16),
            pltpu.VMEM((NARROW, 2, share, 2 * side, depth), jnp.bfloat16),
            pltpu.VMEM((pieces, side, side), jnp.bfloat16),
            pltpu.VMEM((2, 2, HALVES, side, side), jnp.bfloat16),
            pltpu.VMEM((2, 2 * side, width), jnp.float32),
            dma((1 + PARTS,)),
            dma((pieces,)),
            dma((pieces,)),
            dma((pieces,)),
            dma((pieces,)),
            dma((NARROW, 2, share)),
            dma((2, 2, share)),
            dma((2, share)),
            dma((2, 2, HALVES)),
            dma((NARROW, HALVES)),
        ],
        compiler_params=pltpu.CompilerParams(
            collective_id=0, has_side_effects=True, vmem_limit_bytes=60 * 2**20
        ),
    )(
        a_blocks,
        jnp.transpose(a_cols, (0, 2, 1)),
        jnp.transpose(a_scales, (0, 2, 1)),
        a_counts,
        b_panel,
        b_scales,
        jnp.transpose(keep_mask),
        row_perm,
    )


def shifted(block, axis, distance):
    devices = range(lax.axis_size(axis))
    route = [((i - distance) % len(devices), i) for i in devices]
    return lax.ppermute(block, axis, route)


def chosen(table, index):
    tail = (1,) * (table.ndim - 1)
    index = index.reshape(index.shape + tail)
    found = jnp.broadcast_to(table[0], index.shape[: index.ndim - len(tail)] + table.shape[1:])
    for k in range(1, table.shape[0]):
        found = jnp.where(index == k, table[k], found)
    return found


def section_term(row_blocks, slot_cols, weights, b_tiles):
    row_count = row_blocks.shape[0]
    slot_count = row_blocks.shape[1]
    block_side = row_blocks.shape[2]
    scaled = (row_blocks.astype(jnp.float32) * weights[:, :, None, None]).astype(jnp.bfloat16)
    left = jnp.transpose(scaled, (0, 2, 1, 3)).reshape(
        row_count, block_side, slot_count * block_side
    )
    right = chosen(b_tiles, slot_cols.reshape(-1)).reshape(
        row_count, slot_count * block_side, b_tiles.shape[2]
    )
    return jnp.einsum("rik,rkj->rij", left, right, preferred_element_type=jnp.float32)


def by_rings(a_blocks, a_cols, a_scales, a_counts, b_panel, b_scales, keep_mask, row_perm):
    wide_count = lax.axis_size("wide")
    narrow_count = lax.axis_size("narrow")
    device_row = lax.axis_index("wide")
    device_column = lax.axis_index("narrow")
    row_count, section_share, slot_count, block_side = a_blocks.shape[:4]
    section_total = section_share * narrow_count
    k_rows = b_panel.shape[0] // block_side
    out_width = b_panel.shape[1]
    col_blocks = out_width // block_side
    held = [a_blocks]
    for _ in range(narrow_count - 1):
        held.append(shifted(held[-1], "narrow", 1))
    held = jnp.stack(held)
    slot_ids = jnp.arange(slot_count, dtype=jnp.int32)
    accumulated = jnp.zeros((row_count, block_side, out_width), jnp.float32)
    current = b_panel.reshape(k_rows, block_side, out_width)
    for step_number in range(section_total):
        if step_number > 0:
            current = shifted(current, "wide", 1)
        back = (device_column - step_number // section_share) % narrow_count
        row_blocks = lax.dynamic_index_in_dim(held, back, keepdims=False)
        row_blocks = row_blocks[:, step_number % section_share]
        panel_number = (device_row - step_number) % wide_count
        slot_cols = a_cols[:, step_number]
        live_slots = (slot_ids[None, :] < a_counts[:, step_number][:, None]).astype(jnp.float32)
        weights = (
            a_scales[:, step_number]
            * chosen(lax.dynamic_slice(b_scales, (panel_number * k_rows,), (k_rows,)), slot_cols)
            * live_slots
        )
        accumulated = accumulated + section_term(row_blocks, slot_cols, weights, current)
    masked = (
        accumulated.reshape(row_count, block_side, col_blocks, block_side)
        * keep_mask.astype(jnp.float32)[:, None, :, None]
    )
    filtered = masked.astype(jnp.bfloat16).reshape(row_count, block_side, out_width)
    new_order = row_perm[0]
    positions = jnp.arange(row_count, dtype=jnp.int32)
    matches = (new_order[None, :] == positions[:, None]).astype(jnp.int32)
    inverse = jnp.sum(positions[None, :] * matches, axis=1)
    reordered = chosen(filtered, inverse).reshape(row_count * block_side, out_width)
    return lax.all_to_all(reordered, "narrow", split_axis=0, concat_axis=1, tiled=True)


def per_device(*operands):
    wide_count = lax.axis_size("wide")
    narrow_count = lax.axis_size("narrow")
    rows, share, slots, side = operands[0].shape[:4]
    depth, width = operands[4].shape
    fits = rows == 4 and share == 2 and depth == width == 2 * side
    if fits and narrow_count == NARROW and wide_count == WIDE:
        return fused(*operands)
    return by_rings(*operands)


def solution(mesh):
    in_specs = (
        P("wide", "narrow", None, None, None),
        P("wide", None, None),
        P("wide", None, None),
        P("wide", None),
        P("wide", "narrow"),
        P(),
        P("wide", "narrow"),
        P("wide", None),
    )
    out_specs = P(("wide", "narrow"), None)
    return jax.shard_map(
        per_device, mesh=mesh, in_specs=in_specs, out_specs=out_specs, check_vma=False
    )
```

time: 25.1 us -> 24.1 us (0.960)
  Pallas kernels: 24.1 us -> 23.3 us
    pallas_call x1, Pallas kernels: 24.1 us -> 23.3 us  [fused(): pl.pallas_call(kernel, out_shape=pltpu.VMEM((side, width * NARROW), jnp.b...]
where the time goes in v2:
time: 24.1 us; the launch traced here: 24 us
  Pallas kernels  23.3 us (97%)
  local copies, waits for them, and re-layouts  0.71 us (3%)
    pallas_call x1, Pallas kernels, fused(): pl.pallas_call(kernel, out_shape=pltpu.VMEM((side, width * NARROW), jnp.b...  23.3 us
    unnamed x1, local copies, waits for them, and re-layouts  0.71 us

profile of v2, /device:TPU:0, one launch (start us, length us, event | category | flops | bytes accessed | tf_op | source)
XLA Modules:
  0.0 24.0 jit_solution(14553361738352535923)
XLA Ops:
  0.0 23.3 %shard_map.82 = bf16[128,1024]{1,0:T(8,128)(2,1)S(1)} custom-call(bf16[4,2,2,128,128]{4,3,2,1,0:T(8,128)(2,1)} %a_hbm.1, s32[4,2,8]{2,1,0:T(2,128)} %bitcast.3, f32[4,2,8]{2,1,0:T(2,128)} %bitcast.4, s32[4,8]{1,0:T(4,128)} %counts_hbm.1, bf16[256,256]{1,0:T(8,128)(2,1)} %b_hbm.1, f32[16]{0:T(128)} %b_scales_hbm.1, s32[2,4]{1,0:T(2,128)} %bitcast.5, ...), custom_call_target="tpu_custom_call" | custom-call | tf_op jit(solution)/shard_map/pallas_call | solution.py:388
  23.3 0.7 %copy.10 = bf16[128,1024]{1,0:T(8,128)(2,1)} copy(bf16[128,1024]{1,0:T(8,128)(2,1)S(1)} %shard_map.82) | data formatting | bytes 524288

commit v3 on v2

--- a/solution.py
+++ b/solution.py
@@ -10,6 +10,7 @@
 MESH = pl.DeviceIdType.MESH
 HALVES = 2
 PARTS = 4
+LAG = 1
 WIDE = 8
 DEPTH = 4
 NARROW = 4
@@ -36,6 +37,7 @@
     a_own,
     left,
     right,
+    carry,
     result,
     total,
     load_sem,
@@ -43,6 +45,9 @@
     b_up,
     b_down,
     b_cross,
+    k_recv,
+    k_down,
+    k_mate,
     a_recv,
     a_mate,
     a_far,
@@ -75,6 +80,14 @@
     def _():
         pl.semaphore_signal(barrier, inc=1, device_id=(w + 2, n), device_id_type=MESH)
 
+    @pl.when((z == DEPTH - 2) & (core == 1))
+    def _():
+        pl.semaphore_signal(barrier, inc=1, device_id=(w + 2, mate), device_id_type=MESH)
+
+    @pl.when((z == 0) & (core == 0))
+    def _():
+        pl.semaphore_signal(barrier, inc=1, device_id=(across, mate), device_id_type=MESH)
+
     tables = [
         pltpu.make_async_copy(source, kept, table_sem.at[i])
         for i, (source, kept) in enumerate(
@@ -121,6 +134,34 @@
 
     def crossing(slot):
         return piece(slot, b_cross, across)
+
+    def top_slot(t):
+        return (2 * (DEPTH - 1) + x) * PARTS + t
+
+    def lift(t, source, target, sent, landed, wide, narrow):
+        return pltpu.make_async_remote_copy(
+            src_ref=source,
+            dst_ref=target,
+            send_sem=sent,
+            recv_sem=landed,
+            device_id=(wide, narrow),
+            device_id_type=MESH,
+        )
+
+    def enter(t):
+        slot = w * PARTS + t
+        return lift(t, right.at[slot], carry.at[t], b_down.at[slot], k_recv.at[t], w - 2, mate)
+
+    def carry_down(t):
+        return lift(t, carry.at[t], carry.at[t], k_down.at[t], k_recv.at[t], w - 2, n)
+
+    def carry_mate(t):
+        slot = top_slot(t)
+        return lift(t, carry.at[t], right.at[slot], k_mate.at[t], b_recv.at[slot], w, mate)
+
+    def carry_cross(t):
+        slot = top_slot(t)
+        return lift(t, carry.at[t], right.at[slot], k_down.at[t], b_recv.at[slot], across, mate)
 
     def block(origin, pair, j, sent, target):
         return pltpu.make_async_remote_copy(
@@ -182,7 +223,8 @@
         copy.wait()
 
     neighbours = jnp.where(z > 0, 1, 0) + jnp.where(z < DEPTH - 1, 1, 0)
-    pl.semaphore_wait(barrier, 4 + neighbours)
+    lifted = ((z == DEPTH - 1) & (core == 0)) | ((z == 0) & (core == 1))
+    pl.semaphore_wait(barrier, 4 + neighbours + jnp.where(lifted, 1, 0))
 
     for unit in units[:EARLY]:
         to_far(*unit).start()
@@ -194,9 +236,13 @@
         def _():
             upward(own).start()
 
-        @pl.when(z > 0)
+        @pl.when((z > 0) & ((z < DEPTH - 1) | (core == 1)))
         def _():
             downward(own).start()
+
+        @pl.when((z == DEPTH - 1) & (core == 0))
+        def _():
+            enter(t).start()
 
     for unit in units[:EARLY]:
         to_mate(*unit).start()
@@ -223,11 +269,23 @@
         def _():
             downward(from_above).wait_recv()
 
-            @pl.when(z > 0)
+            @pl.when((z > 0) & ((z + step < DEPTH - 1) | (core == 1)))
             def _():
                 downward(from_above).start()
 
-            crossing(from_above).start()
+            @pl.when((z > 0) | (step < DEPTH - 1) | (core == 1))
+            def _():
+                crossing(from_above).start()
+
+    def ferry(step, t):
+        @pl.when((z + step == DEPTH - 1) & (core == 1))
+        def _():
+            carry_down(t).wait_recv()
+            if step < DEPTH - 1:
+                carry_down(t).start()
+            else:
+                carry_cross(t).start()
+            carry_mate(t).start()
 
     def hand_over(pair, j):
         from_far(pair, j).wait_recv()
@@ -284,26 +342,32 @@
 
     for t in range(PARTS):
         relay(1, t)
+        if t >= LAG:
+            ferry(1, t - LAG)
+    for t in range(PARTS - LAG, PARTS):
+        ferry(1, t)
     hand_over(give, 0)
-    relay(2, 0)
-    relay(2, 1)
-    hand_over(give, 1)
-    relay(2, 2)
-    relay(2, 3)
+    for t in range(PARTS):
+        ferry(2, t)
+        relay(2, t)
+        if t == 1:
+            hand_over(give, 1)
     mate_arrived(give, 0)
     mate_arrived(give, 1)
     diagonal_arrived(give, 0)
     add(0, give, [(0, 0), (0, 1), (0, 2)], first=True)
-    relay(3, 0)
-    relay(3, 1)
+    for t in range(PARTS // 2):
+        ferry(3, t)
+        relay(3, t)
     diagonal_arrived(give, 1)
     for level in range(2):
         for h in range(HALVES):
             peer_arrived(near[level], h)
     add(0, give, [(1, 0), (1, 1)])
     hand_over(hold, 0)
-    relay(3, 2)
-    relay(3, 3)
+    for t in range(PARTS // 2, PARTS):
+        ferry(3, t)
+        relay(3, t)
     add(0, give, [(0, 3)])
     for h in range(HALVES):
         peer_arrived(near[2], h)
@@ -313,6 +377,8 @@
     diagonal_arrived(hold, 0)
     add(1, hold, [(0, 0), (0, 1), (0, 2), (0, 3)], first=True)
     for h in range(HALVES):
+        if h == 1:
+            hand_over(hold, 1)
         peer_arrived(near[3], h)
         value = total[0, :, h * side : (h + 1) * side] + term(give, 1, near[3], h)
         for c in range(2):
@@ -320,7 +386,6 @@
             kept = value[c * side : (c + 1) * side] * keep[h, home(q)].astype(jnp.float32)
             result[0, c, h] = kept.astype(jnp.bfloat16)
             deliver(c, h, 0, q).start()
-    hand_over(hold, 1)
     diagonal_arrived(hold, 1)
     add(1, hold, [(1, 0), (1, 1), (1, 2), (1, 3)])
     for h in range(HALVES):
@@ -352,15 +417,23 @@
 
                 crossing(from_below).wait_send()
 
-            @pl.when((z + step < DEPTH) & (z > 0))
+            passed = (z + step < DEPTH - 1) | (core == 1) | (step == 0)
+
+            @pl.when((z + step < DEPTH) & (z > 0) & passed)
             def _():
                 downward(from_above).wait_send()
 
             if step > 0:
 
-                @pl.when(z + step < DEPTH)
+                @pl.when((z + step < DEPTH) & ((z > 0) | (step < DEPTH - 1) | (core == 1)))
                 def _():
                     crossing(from_above).wait_send()
+
+    @pl.when((z < DEPTH - 1) & (core == 1))
+    def _():
+        for t in range(PARTS):
+            carry_down(t).wait_send()
+            carry_mate(t).wait_send()
 
     for h in range(HALVES):
         for c in range(2):
@@ -401,6 +474,7 @@
             pltpu.VMEM(a_blocks.shape, jnp.bfloat16),
             pltpu.VMEM((NARROW, 2, share, 2 * side, depth), jnp.bfloat16),
             pltpu.VMEM((pieces, side, side), jnp.bfloat16),
+            pltpu.VMEM((PARTS, side, side), jnp.bfloat16),
             pltpu.VMEM((2, 2, HALVES, side, side), jnp.bfloat16),
             pltpu.VMEM((2, 2 * side, width), jnp.float32),
             dma((1 + PARTS,)),
@@ -408,6 +482,9 @@
             dma((pieces,)),
             dma((pieces,)),
             dma((pieces,)),
+            dma((PARTS,)),
+            dma((PARTS,)),
+            dma((PARTS,)),
             dma((NARROW, 2, share)),
             dma((2, 2, share)),
             dma((2, share)),

time: 24.1 us -> 23.6 us (0.979)
  Pallas kernels: 23.3 us -> 22.7 us
    pallas_call x1, Pallas kernels: 23.3 us -> 22.7 us  [fused(): pl.pallas_call(kernel, out_shape=pltpu.VMEM((side, width * NARROW), jnp.b...]
where the time goes in v3:
time: 23.6 us; the launch traced here: 23.4 us
  Pallas kernels  22.7 us (96%)
  local copies, waits for them, and re-layouts  0.71 us (3%)
    pallas_call x1, Pallas kernels, fused(): pl.pallas_call(kernel, out_shape=pltpu.VMEM((side, width * NARROW), jnp.b...  22.7 us
    unnamed x1, local copies, waits for them, and re-layouts  0.71 us

profile of v3, /device:TPU:0, one launch (start us, length us, event | category | flops | bytes accessed | tf_op | source)
XLA Modules:
  0.0 23.4 jit_solution(17454997447671450064)
XLA Ops:
  0.0 22.7 %shard_map.82 = bf16[128,1024]{1,0:T(8,128)(2,1)S(1)} custom-call(bf16[4,2,2,128,128]{4,3,2,1,0:T(8,128)(2,1)} %a_hbm.1, s32[4,2,8]{2,1,0:T(2,128)} %bitcast.3, f32[4,2,8]{2,1,0:T(2,128)} %bitcast.4, s32[4,8]{1,0:T(4,128)} %counts_hbm.1, bf16[256,256]{1,0:T(8,128)(2,1)} %b_hbm.1, f32[16]{0:T(128)} %b_scales_hbm.1, s32[2,4]{1,0:T(2,128)} %bitcast.5, ...), custom_call_target="tpu_custom_call" | custom-call | tf_op jit(solution)/shard_map/pallas_call | solution.py:461
  22.7 0.7 %copy.10 = bf16[128,1024]{1,0:T(8,128)(2,1)} copy(bf16[128,1024]{1,0:T(8,128)(2,1)S(1)} %shard_map.82) | data formatting | bytes 524288

commit v4 on v3

--- a/solution.py
+++ b/solution.py
@@ -120,7 +120,7 @@
         return pltpu.make_async_remote_copy(
             src_ref=right.at[slot],
             dst_ref=right.at[slot],
-            send_sem=sent.at[slot],
+            send_sem=sent.at[0],
             recv_sem=b_recv.at[slot],
             device_id=(target, n),
             device_id_type=MESH,
@@ -150,18 +150,18 @@
 
     def enter(t):
         slot = w * PARTS + t
-        return lift(t, right.at[slot], carry.at[t], b_down.at[slot], k_recv.at[t], w - 2, mate)
+        return lift(t, right.at[slot], carry.at[t], b_down.at[0], k_recv.at[t], w - 2, mate)
 
     def carry_down(t):
-        return lift(t, carry.at[t], carry.at[t], k_down.at[t], k_recv.at[t], w - 2, n)
+        return lift(t, carry.at[t], carry.at[t], k_down.at[0], k_recv.at[t], w - 2, n)
 
     def carry_mate(t):
         slot = top_slot(t)
-        return lift(t, carry.at[t], right.at[slot], k_mate.at[t], b_recv.at[slot], w, mate)
+        return lift(t, carry.at[t], right.at[slot], k_mate.at[0], b_recv.at[slot], w, mate)
 
     def carry_cross(t):
         slot = top_slot(t)
-        return lift(t, carry.at[t], right.at[slot], k_down.at[t], b_recv.at[slot], across, mate)
+        return lift(t, carry.at[t], right.at[slot], k_down.at[0], b_recv.at[slot], across, mate)
 
     def block(origin, pair, j, sent, target):
         return pltpu.make_async_remote_copy(
@@ -174,16 +174,16 @@
         )
 
     def to_far(pair, j):
-        return block(n, pair, j, a_far.at[pair, j], far)
+        return block(n, pair, j, a_far.at[0], far)
 
     def to_mate(pair, j):
-        return block(n, pair, j, a_mate.at[0, pair, j], mate)
+        return block(n, pair, j, a_mate.at[0], mate)
 
     def from_far(pair, j):
-        return block(far, pair, j, a_far.at[pair, j], far)
+        return block(far, pair, j, a_far.at[0], far)
 
     def pass_on(pair, j):
-        return block(far, pair, j, a_mate.at[1, pair, j], mate)
+        return block(far, pair, j, a_mate.at[1], mate)
 
     def home(q):
         found = jnp.int32(0)
@@ -226,23 +226,30 @@
     lifted = ((z == DEPTH - 1) & (core == 0)) | ((z == 0) & (core == 1))
     pl.semaphore_wait(barrier, 4 + neighbours + jnp.where(lifted, 1, 0))
 
+    @pl.when((z == DEPTH - 1) & (core == 0))
+    def _():
+        for t in range(PARTS):
+            enter(t).start()
+
+    @pl.when((z == DEPTH - 1) & (core == 1))
+    def _():
+        for t in range(PARTS):
+            downward(w * PARTS + t).start()
+
     for unit in units[:EARLY]:
         to_far(*unit).start()
     for t in range(PARTS):
         own = w * PARTS + t
-        crossing(own).start()
 
         @pl.when(z < DEPTH - 1)
         def _():
             upward(own).start()
 
-        @pl.when((z > 0) & ((z < DEPTH - 1) | (core == 1)))
+        @pl.when((z > 0) & (z < DEPTH - 1))
         def _():
             downward(own).start()
 
-        @pl.when((z == DEPTH - 1) & (core == 0))
-        def _():
-            enter(t).start()
+        crossing(own).start()
 
     for unit in units[:EARLY]:
         to_mate(*unit).start()
@@ -292,10 +299,10 @@
         pass_on(pair, j).start()
 
     def mate_arrived(pair, j):
-        block(mate, pair, j, a_mate.at[0, pair, j], mate).wait_recv()
+        block(mate, pair, j, a_mate.at[0], mate).wait_recv()
 
     def diagonal_arrived(pair, j):
-        block(diagonal, pair, j, a_mate.at[1, pair, j], mate).wait_recv()
+        block(diagonal, pair, j, a_mate.at[1], mate).wait_recv()
 
     near = (
         z,
@@ -334,7 +341,7 @@
         return pltpu.make_async_remote_copy(
             src_ref=result.at[source, c, h],
             dst_ref=out.at[:, pl.ds(start, side)],
-            send_sem=r_send.at[source, c, h],
+            send_sem=r_send.at[source],
             recv_sem=r_recv.at[n, h],
             device_id=(w, target),
             device_id_type=MESH,
@@ -372,10 +379,6 @@
     for h in range(HALVES):
         peer_arrived(near[2], h)
     add(0, give, [(1, 2)])
-    mate_arrived(hold, 0)
-    mate_arrived(hold, 1)
-    diagonal_arrived(hold, 0)
-    add(1, hold, [(0, 0), (0, 1), (0, 2), (0, 3)], first=True)
     for h in range(HALVES):
         if h == 1:
             hand_over(hold, 1)
@@ -386,6 +389,10 @@
             kept = value[c * side : (c + 1) * side] * keep[h, home(q)].astype(jnp.float32)
             result[0, c, h] = kept.astype(jnp.bfloat16)
             deliver(c, h, 0, q).start()
+    mate_arrived(hold, 0)
+    mate_arrived(hold, 1)
+    diagonal_arrived(hold, 0)
+    add(1, hold, [(0, 0), (0, 1), (0, 2), (0, 3)], first=True)
     diagonal_arrived(hold, 1)
     add(1, hold, [(1, 0), (1, 1), (1, 2), (1, 3)])
     for h in range(HALVES):
@@ -400,52 +407,43 @@
             jnp.bfloat16
         )
 
-    for unit in units:
-        to_far(*unit).wait_send()
-        to_mate(*unit).wait_send()
-        pass_on(*unit).wait_send()
-    for t in range(PARTS):
-        for step in range(DEPTH):
-            from_below = (w - 2 * step) * PARTS + t
-            from_above = (w + 2 * step) * PARTS + t
-
-            @pl.when(z - step >= 0)
-            def _():
-                @pl.when(z < DEPTH - 1)
-                def _():
-                    upward(from_below).wait_send()
-
-                crossing(from_below).wait_send()
-
-            passed = (z + step < DEPTH - 1) | (core == 1) | (step == 0)
-
-            @pl.when((z + step < DEPTH) & (z > 0) & passed)
-            def _():
-                downward(from_above).wait_send()
-
-            if step > 0:
-
-                @pl.when((z + step < DEPTH) & ((z > 0) | (step < DEPTH - 1) | (core == 1)))
-                def _():
-                    crossing(from_above).wait_send()
-
-    @pl.when((z < DEPTH - 1) & (core == 1))
-    def _():
-        for t in range(PARTS):
-            carry_down(t).wait_send()
-            carry_mate(t).wait_send()
-
-    for h in range(HALVES):
+    def drain(source, sem):
+        pltpu.make_async_remote_copy(
+            src_ref=source,
+            dst_ref=source,
+            send_sem=sem,
+            recv_sem=b_recv.at[0],
+            device_id=(w, mate),
+            device_id_type=MESH,
+        ).wait_send()
+
+    for sem in (a_far.at[0], a_mate.at[0], a_mate.at[1]):
+        drain(left.at[n], sem)
+    for k in range(DEPTH):
         for c in range(2):
-            deliver(c, h, 0, 2 * give + c).wait_send()
-        deliver(0, h, 1, mate).wait_send()
+
+            @pl.when((z == k) & (core == c))
+            def _(k=k, c=c):
+                if k < DEPTH - 1:
+                    drain(right.at[pl.ds(0, PARTS * (k + 1))], b_up.at[0])
+                if k > 0:
+                    levels = DEPTH - k if c == 1 else max(DEPTH - 1 - k, 1)
+                    drain(right.at[pl.ds(0, PARTS * levels)], b_down.at[0])
+                levels = DEPTH if c == 1 or k > 0 else DEPTH - 1
+                drain(right.at[pl.ds(0, PARTS * levels)], b_cross.at[0])
+                if c == 1 and k < DEPTH - 1:
+                    drain(right.at[pl.ds(0, PARTS)], k_down.at[0])
+                    drain(right.at[pl.ds(0, PARTS)], k_mate.at[0])
+
+    drain(result.at[0], r_send.at[0])
+    drain(result.at[1, 0], r_send.at[1])
     for origin in (mate, far, diagonal):
         for h in range(HALVES):
             start = pl.multiple_of(origin * width + h * side, side)
             pltpu.make_async_remote_copy(
                 src_ref=result.at[0, 0, h],
                 dst_ref=out.at[:, pl.ds(start, side)],
-                send_sem=r_send.at[0, 0, h],
+                send_sem=r_send.at[0],
                 recv_sem=r_recv.at[origin, h],
                 device_id=(w, origin),
                 device_id_type=MESH,
@@ -479,16 +477,16 @@
             pltpu.VMEM((2, 2 * side, width), jnp.float32),
             dma((1 + PARTS,)),
             dma((pieces,)),
-            dma((pieces,)),
-            dma((pieces,)),
-            dma((pieces,)),
+            dma((1,)),
+            dma((1,)),
+            dma((1,)),
             dma((PARTS,)),
-            dma((PARTS,)),
-            dma((PARTS,)),
+            dma((1,)),
+            dma((1,)),
             dma((NARROW, 2, share)),
-            dma((2, 2, share)),
-            dma((2, share)),
-            dma((2, 2, HALVES)),
+            dma((2,)),
+            dma((1,)),
+            dma((2,)),
             dma((NARROW, HALVES)),
         ],
         compiler_params=pltpu.CompilerParams(

time: 23.6 us -> 22.5 us (0.953)
  Pallas kernels: 22.7 us -> 21.6 us
    pallas_call x1, Pallas kernels: 22.7 us -> 21.6 us  [fused(): pl.pallas_call(kernel, out_shape=pltpu.VMEM((side, width * NARROW), jnp.b...]
where the time goes in v4:
time: 22.5 us; the launch traced here: 22.3 us
  Pallas kernels  21.6 us (96%)
  local copies, waits for them, and re-layouts  0.71 us (3%)
    pallas_call x1, Pallas kernels, fused(): pl.pallas_call(kernel, out_shape=pltpu.VMEM((side, width * NARROW), jnp.b...  21.6 us
    unnamed x1, local copies, waits for them, and re-layouts  0.71 us

profile of v4, /device:TPU:0, one launch (start us, length us, event | category | flops | bytes accessed | tf_op | source)
XLA Modules:
  0.0 22.3 jit_solution(3252260627941127092)
XLA Ops:
  0.0 21.6 %shard_map.82 = bf16[128,1024]{1,0:T(8,128)(2,1)S(1)} custom-call(bf16[4,2,2,128,128]{4,3,2,1,0:T(8,128)(2,1)} %a_hbm.1, s32[4,2,8]{2,1,0:T(2,128)} %bitcast.3, f32[4,2,8]{2,1,0:T(2,128)} %bitcast.4, s32[4,8]{1,0:T(4,128)} %counts_hbm.1, bf16[256,256]{1,0:T(8,128)(2,1)} %b_hbm.1, f32[16]{0:T(128)} %b_scales_hbm.1, s32[2,4]{1,0:T(2,128)} %bitcast.5, ...), custom_call_target="tpu_custom_call" | custom-call | tf_op jit(solution)/shard_map/pallas_call | solution.py:459
  21.6 0.7 %copy.10 = bf16[128,1024]{1,0:T(8,128)(2,1)} copy(bf16[128,1024]{1,0:T(8,128)(2,1)S(1)} %shard_map.82) | data formatting | bytes 524288

commit v5 on v4

--- a/solution.py
+++ b/solution.py
@@ -375,15 +375,14 @@
     for t in range(PARTS // 2, PARTS):
         ferry(3, t)
         relay(3, t)
-    add(0, give, [(0, 3)])
-    for h in range(HALVES):
-        peer_arrived(near[2], h)
-    add(0, give, [(1, 2)])
     for h in range(HALVES):
         if h == 1:
             hand_over(hold, 1)
+        peer_arrived(near[2], h)
+        value = total[0, :, h * side : (h + 1) * side] + term(give, 0, near[3], h)
+        value = value + term(give, 1, near[2], h)
         peer_arrived(near[3], h)
-        value = total[0, :, h * side : (h + 1) * side] + term(give, 1, near[3], h)
+        value = value + term(give, 1, near[3], h)
         for c in range(2):
             q = 2 * give + c
             kept = value[c * side : (c + 1) * side] * keep[h, home(q)].astype(jnp.float32)

time: 22.5 us -> 22.5 us (level)
  no operation moved by 1% of the time
where the time goes in v5:
time: 22.5 us; the launch traced here: 22.3 us
  Pallas kernels  21.6 us (96%)
  local copies, waits for them, and re-layouts  0.71 us (3%)
    pallas_call x1, Pallas kernels, fused(): pl.pallas_call(kernel, out_shape=pltpu.VMEM((side, width * NARROW), jnp.b...  21.6 us
    unnamed x1, local copies, waits for them, and re-layouts  0.71 us

profile of v5, /device:TPU:0, one launch (start us, length us, event | category | flops | bytes accessed | tf_op | source)
XLA Modules:
  0.0 22.3 jit_solution(17112605545774689178)
XLA Ops:
  0.0 21.6 %shard_map.82 = bf16[128,1024]{1,0:T(8,128)(2,1)S(1)} custom-call(bf16[4,2,2,128,128]{4,3,2,1,0:T(8,128)(2,1)} %a_hbm.1, s32[4,2,8]{2,1,0:T(2,128)} %bitcast.3, f32[4,2,8]{2,1,0:T(2,128)} %bitcast.4, s32[4,8]{1,0:T(4,128)} %counts_hbm.1, bf16[256,256]{1,0:T(8,128)(2,1)} %b_hbm.1, f32[16]{0:T(128)} %b_scales_hbm.1, s32[2,4]{1,0:T(2,128)} %bitcast.5, ...), custom_call_target="tpu_custom_call" | custom-call | tf_op jit(solution)/shard_map/pallas_call | solution.py:458
  21.6 0.7 %copy.10 = bf16[128,1024]{1,0:T(8,128)(2,1)} copy(bf16[128,1024]{1,0:T(8,128)(2,1)S(1)} %shard_map.82) | data formatting | bytes 524288

commit v6 on v5

--- a/solution.py
+++ b/solution.py
@@ -376,8 +376,6 @@
         ferry(3, t)
         relay(3, t)
     for h in range(HALVES):
-        if h == 1:
-            hand_over(hold, 1)
         peer_arrived(near[2], h)
         value = total[0, :, h * side : (h + 1) * side] + term(give, 0, near[3], h)
         value = value + term(give, 1, near[2], h)
@@ -388,6 +386,7 @@
             kept = value[c * side : (c + 1) * side] * keep[h, home(q)].astype(jnp.float32)
             result[0, c, h] = kept.astype(jnp.bfloat16)
             deliver(c, h, 0, q).start()
+    hand_over(hold, 1)
     mate_arrived(hold, 0)
     mate_arrived(hold, 1)
     diagonal_arrived(hold, 0)

time: 22.5 us -> 22.5 us (level)
  no operation moved by 1% of the time
where the time goes in v6:
time: 22.5 us; the launch traced here: 22.3 us
  Pallas kernels  21.6 us (96%)
  local copies, waits for them, and re-layouts  0.71 us (3%)
    pallas_call x1, Pallas kernels, fused(): pl.pallas_call(kernel, out_shape=pltpu.VMEM((side, width * NARROW), jnp.b...  21.6 us
    unnamed x1, local copies, waits for them, and re-layouts  0.71 us

profile of v6, /device:TPU:0, one launch (start us, length us, event | category | flops | bytes accessed | tf_op | source)
XLA Modules:
  0.0 22.3 jit_solution(17959484073908941961)
XLA Ops:
  0.0 21.6 %shard_map.82 = bf16[128,1024]{1,0:T(8,128)(2,1)S(1)} custom-call(bf16[4,2,2,128,128]{4,3,2,1,0:T(8,128)(2,1)} %a_hbm.1, s32[4,2,8]{2,1,0:T(2,128)} %bitcast.3, f32[4,2,8]{2,1,0:T(2,128)} %bitcast.4, s32[4,8]{1,0:T(4,128)} %counts_hbm.1, bf16[256,256]{1,0:T(8,128)(2,1)} %b_hbm.1, f32[16]{0:T(128)} %b_scales_hbm.1, s32[2,4]{1,0:T(2,128)} %bitcast.5, ...), custom_call_target="tpu_custom_call" | custom-call | tf_op jit(solution)/shard_map/pallas_call | solution.py:457
  21.6 0.7 %copy.10 = bf16[128,1024]{1,0:T(8,128)(2,1)} copy(bf16[128,1024]{1,0:T(8,128)(2,1)S(1)} %shard_map.82) | data formatting | bytes 524288

commit v7 on v6

--- a/solution.py
+++ b/solution.py
@@ -342,7 +342,7 @@
             src_ref=result.at[source, c, h],
             dst_ref=out.at[:, pl.ds(start, side)],
             send_sem=r_send.at[source],
-            recv_sem=r_recv.at[n, h],
+            recv_sem=r_recv.at[n],
             device_id=(w, target),
             device_id_type=MESH,
         )
@@ -436,16 +436,15 @@
     drain(result.at[0], r_send.at[0])
     drain(result.at[1, 0], r_send.at[1])
     for origin in (mate, far, diagonal):
-        for h in range(HALVES):
-            start = pl.multiple_of(origin * width + h * side, side)
-            pltpu.make_async_remote_copy(
-                src_ref=result.at[0, 0, h],
-                dst_ref=out.at[:, pl.ds(start, side)],
-                send_sem=r_send.at[0],
-                recv_sem=r_recv.at[origin, h],
-                device_id=(w, origin),
-                device_id_type=MESH,
-            ).wait_recv()
+        place = out.at[:, pl.ds(pl.multiple_of(origin * width, width), width)]
+        pltpu.make_async_remote_copy(
+            src_ref=place,
+            dst_ref=place,
+            send_sem=r_send.at[0],
+            recv_sem=r_recv.at[origin],
+            device_id=(w, origin),
+            device_id_type=MESH,
+        ).wait_recv()
 
 
 def fused(a_blocks, a_cols, a_scales, a_counts, b_panel, b_scales, keep_mask, row_perm):
@@ -485,7 +484,7 @@
             dma((2,)),
             dma((1,)),
             dma((2,)),
-            dma((NARROW, HALVES)),
+            dma((NARROW,)),
         ],
         compiler_params=pltpu.CompilerParams(
             collective_id=0, has_side_effects=True, vmem_limit_bytes=60 * 2**20

time: 22.5 us -> 22.4 us (level)
  no operation moved by 1% of the time
where the time goes in v7:
time: 22.4 us; the launch traced here: 22.3 us
  Pallas kernels  21.6 us (96%)
  local copies, waits for them, and re-layouts  0.71 us (3%)
    pallas_call x1, Pallas kernels, fused(): pl.pallas_call(kernel, out_shape=pltpu.VMEM((side, width * NARROW), jnp.b...  21.6 us
    unnamed x1, local copies, waits for them, and re-layouts  0.71 us

profile of v7, /device:TPU:0, one launch (start us, length us, event | category | flops | bytes accessed | tf_op | source)
XLA Modules:
  0.0 22.3 jit_solution(10625657147245856200)
XLA Ops:
  0.0 21.6 %shard_map.82 = bf16[128,1024]{1,0:T(8,128)(2,1)S(1)} custom-call(bf16[4,2,2,128,128]{4,3,2,1,0:T(8,128)(2,1)} %a_hbm.1, s32[4,2,8]{2,1,0:T(2,128)} %bitcast.3, f32[4,2,8]{2,1,0:T(2,128)} %bitcast.4, s32[4,8]{1,0:T(4,128)} %counts_hbm.1, bf16[256,256]{1,0:T(8,128)(2,1)} %b_hbm.1, f32[16]{0:T(128)} %b_scales_hbm.1, s32[2,4]{1,0:T(2,128)} %bitcast.5, ...), custom_call_target="tpu_custom_call" | custom-call | tf_op jit(solution)/shard_map/pallas_call | solution.py:456
  21.6 0.7 %copy.10 = bf16[128,1024]{1,0:T(8,128)(2,1)} copy(bf16[128,1024]{1,0:T(8,128)(2,1)S(1)} %shard_map.82) | data formatting | bytes 524288

commit v8 on v7

--- a/solution.py
+++ b/solution.py
@@ -10,7 +10,7 @@
 MESH = pl.DeviceIdType.MESH
 HALVES = 2
 PARTS = 4
-LAG = 1
+LAG = 2
 WIDE = 8
 DEPTH = 4
 NARROW = 4

time: 22.4 us -> 22.6 us (level)
  no operation moved by 1% of the time
where the time goes in v8:
time: 22.6 us; the launch traced here: 22.5 us
  Pallas kernels  21.8 us (96%)
  local copies, waits for them, and re-layouts  0.71 us (3%)
    pallas_call x1, Pallas kernels, fused(): pl.pallas_call(kernel, out_shape=pltpu.VMEM((side, width * NARROW), jnp.b...  21.8 us
    unnamed x1, local copies, waits for them, and re-layouts  0.71 us

profile of v8, /device:TPU:0, one launch (start us, length us, event | category | flops | bytes accessed | tf_op | source)
XLA Modules:
  0.0 22.5 jit_solution(11752404447378224242)
XLA Ops:
  0.0 21.8 %shard_map.82 = bf16[128,1024]{1,0:T(8,128)(2,1)S(1)} custom-call(bf16[4,2,2,128,128]{4,3,2,1,0:T(8,128)(2,1)} %a_hbm.1, s32[4,2,8]{2,1,0:T(2,128)} %bitcast.3, f32[4,2,8]{2,1,0:T(2,128)} %bitcast.4, s32[4,8]{1,0:T(4,128)} %counts_hbm.1, bf16[256,256]{1,0:T(8,128)(2,1)} %b_hbm.1, f32[16]{0:T(128)} %b_scales_hbm.1, s32[2,4]{1,0:T(2,128)} %bitcast.5, ...), custom_call_target="tpu_custom_call" | custom-call | tf_op jit(solution)/shard_map/pallas_call | solution.py:456
  21.8 0.7 %copy.10 = bf16[128,1024]{1,0:T(8,128)(2,1)} copy(bf16[128,1024]{1,0:T(8,128)(2,1)S(1)} %shard_map.82) | data formatting | bytes 524288
